TPU v7x, 32 devices: a whole 2x2x4 slice. The times are simulated.
32 devices in a mesh: segment: 2 (over y), lon: 4 (over x, core), lat: 4 (over z).
Axes of the slice: x: 2, y: 2, z: 4, core: 2. Of those that a mesh axis runs over, the one named last changes fastest.
Arguments:
- latents: bfloat16 [2, 24, 48, 1024], P(None, 'lat', 'lon'), may hold values from -48 to 48
- land_mask: int32 [24, 48], P('lat', 'lon'), may hold values 0 or 1
- land_embed: bfloat16 [1024], replicated, may hold values from -6 to 6
- qkv_weight: bfloat16 [2, 1024, 3072], P('segment'), may hold values from -0.25625 to 0.25625
- out_weight: bfloat16 [2, 1024, 1024], P('segment'), may hold values from -0.5625 to 0.5625
- norm_gain: float32 [2, 1024], replicated, may hold values from 0.5 to 1.5
- offsets: int32 [2, 2], replicated, may hold values from 0 to 11, as said below
Outputs:
- sections: bfloat16 [2, 2, 24, 48, 1024], P('segment', None, 'lat', 'lon')
Inputs may be any that keep to these rules, and one draw needn't show every extreme that they name: offsets[s, 0] lies in 0 to 5 and offsets[s, 1] in 0 to 11; one of the two sections has offsets[s, 0] = 5 and offsets[s, 1] = 11.
All inputs are finite; a program needn't handle non-finite values. No bound on the sum of `land_mask` on one device may be relied on, other than what follows from the above.
Results may differ from a plain program's by a relative error of at most 0.015.
Values may be sent and summed in bfloat16 or wider, within the bound.
A program may use at most 64 MiB of HBM per device.

v0:
```python
import functools
import math

import jax
import jax.numpy as jnp
from jax import lax
from jax.experimental import pallas as pl
from jax.experimental.pallas import tpu as pltpu
from jax.sharding import PartitionSpec as P

HEADS = 16
WLAT = 6
WLON = 12
HALF_LAT = WLAT // 2
HALF_LON = WLON // 2
CELLS = WLAT * WLON
HELD = 80
QUAD = 16
PAIR = 128
NT = (((1,), (1,)), ((), ()))
F32 = jnp.float32
BF16 = jnp.bfloat16


def dot(a, b):
    return jnp.dot(a, b, preferred_element_type=F32)


def iota(shape, axis):
    return lax.broadcasted_iota(jnp.int32, shape, axis)


def based(offset, window):
    return jnp.where(offset >= window // 2, offset - window, offset)


def split_by(value, size, count):
    high = sum((value >= size * k).astype(jnp.int32) for k in range(1, count))
    return high, value - size * high


def quarter_cell(t):
    late = t >= 4 * QUAD
    quarter = jnp.where(late, (t - 4 * QUAD) >> 1, t >> 4)
    j = jnp.where(late, QUAD + (t & 1), t & (QUAD - 1))
    row, column = split_by(j, HALF_LON, 3)
    return HALF_LAT * (quarter >> 1) + row, HALF_LON * (quarter & 1) + column


def source(row, column, lat_sign, lon_sign, small):
    row_out = (row < 0) | (row >= WLAT)
    column_out = (column < 0) | (column >= WLON)
    row = jnp.where(row_out, row - WLAT * lat_sign, row)
    column = jnp.where(column_out, column - WLON * lon_sign, column)
    low, near_row = split_by(row, HALF_LAT, 2)
    right, near_column = split_by(column, HALF_LON, 2)
    base = jnp.where(
        row_out,
        jnp.where(column_out, 8 * QUAD, 4 * QUAD + QUAD * right),
        jnp.where(column_out, 6 * QUAD + QUAD * low, 2 * QUAD * low + QUAD * right),
    )
    j = HALF_LON * near_row + near_column
    if small is not None:
        small_base = jnp.where(row_out, jnp.where(column_out, 8 * QUAD, 4 * QUAD), 6 * QUAD)
        small_j = jnp.where(row_out, jnp.where(column_out, QUAD, column), row)
        whole = ~(row_out | column_out) | jnp.logical_not(small)
        base, j = jnp.where(whole, base, small_base), jnp.where(whole, j, small_j)
    return base, j, column_out, column


def choosers(row, column, signs, small, beyond, wanted, pieces, main_ref, tail_ref, far_ref):
    base, j, column_out, column = source(row, column, *signs, small)
    near = wanted
    if beyond is not None:
        lines, line, past = beyond
        near = wanted & jnp.logical_not(past)
        held = wanted & past & (line >= 0) & (line < lines)
        far = QUAD * line + jnp.where(column_out, QUAD * lines, 0) + column
        lane = iota(far_ref.shape, 1)
        far_ref[...] = (lane == jnp.where(held, far, -1000)).astype(F32).astype(BF16)
    base = jnp.where(near, base, -5000)
    count = row.shape[0]
    lane = iota((count, 9 * QUAD), 1)
    main_ref[...] = (lane == jnp.where(j < QUAD, base + j, -1000)).astype(F32).astype(BF16)
    tail = jnp.where(j >= QUAD, base + j - QUAD, -1000)

    def fill(piece, carry):
        start = pl.multiple_of(piece * count, QUAD)
        tail_ref[pl.ds(start, count), :] = (lane == tail + 2 * piece).astype(F32).astype(BF16)
        return carry

    lax.fori_loop(0, pieces, fill, 0)


def gathered(block, far, main_ref, tail_ref, far_ref, width, pieces):
    count = main_ref.shape[0]
    tail = dot(tail_ref[...], block[:, width:])
    tail = jnp.concatenate([tail[p * count : (p + 1) * count] for p in range(pieces)], axis=1)
    tail = dot(main_ref[...], block[:, :width]) + tail
    return tail if far is None else tail + dot(far_ref[...], far)


def store_quarters(cells, ref, level, width, pieces):
    cells = cells[:CELLS].astype(F32)
    piece = width // pieces
    ref[level, pl.ds(0, 4 * QUAD), pl.ds(0, width)] = cells[: 4 * QUAD].astype(BF16)
    stack = jnp.concatenate([cells[4 * QUAD :, p * piece : (p + 1) * piece] for p in range(pieces)], axis=0)
    to, at = iota((4 * QUAD, 8 * pieces), 0), iota((4 * QUAD, 8 * pieces), 1)
    wanted = 8 * ((to & (QUAD - 1)) >> 1) + 2 * (to >> 4) + (to & 1)
    pick = (at == wanted).astype(F32).astype(BF16)
    ref[level, pl.ds(0, 4 * QUAD), pl.ds(width, piece)] = dot(pick, stack.astype(BF16)).astype(BF16)


def store_edges(cells, lat_sign, lon_sign, line_ref, corner_ref, level, pieces):
    row_at, column_at = (0 if lat_sign > 0 else WLAT - 1), (0 if lon_sign > 0 else WLON - 1)
    to = iota((2 * QUAD, CELLS), 0)
    row, column = quarter_cell(iota((2 * QUAD, CELLS), 1))
    pick = ((row == row_at) & (column == to)) | ((column == column_at) & (row == to - QUAD))
    line_ref[level] = dot(pick.astype(F32).astype(BF16), cells[:CELLS].astype(BF16)).astype(BF16)
    half = HALF_LON * (row_at % HALF_LAT) + column_at % HALF_LON
    quarter = 2 * (row_at // HALF_LAT) + column_at // HALF_LON
    place = QUAD * quarter + half if half < QUAD else 4 * QUAD + 2 * quarter + half - QUAD
    piece = cells.shape[1] // pieces
    line = iota((QUAD, piece), 0)
    corner = jnp.zeros((QUAD, piece), F32)
    for p in range(pieces):
        corner = jnp.where(line == 2 * p, cells[place : place + 1, p * piece : (p + 1) * piece], corner)
    corner_ref[level] = corner.astype(BF16)


def seed(entering, latents_ref, mask_ref, embed_ref, pieces, edges, ready):
    levels, width = latents_ref.shape[2:]
    embed = embed_ref[...].astype(F32).reshape(1, width)
    across = WLON * levels
    spread = iota((across, WLON), 0)
    spread = (spread >= levels * iota((across, WLON), 1)) & (spread < levels * iota((across, WLON), 1) + levels)
    rows = []
    for row in range(WLAT):
        land = jnp.where(spread, mask_ref[row : row + 1, :].astype(F32), 0.0)
        land = jnp.sum(land, axis=1, keepdims=True)
        rows.append(latents_ref[row].astype(F32).reshape(across, width) + land * embed)
    cells = jnp.concatenate(rows, axis=0).astype(BF16)
    row, column = quarter_cell(iota((CELLS, CELLS * levels), 0))
    wanted = levels * (WLON * row + column)
    at = iota((CELLS, CELLS * levels), 1)
    for level in range(levels):
        order = (at == wanted + level).astype(F32).astype(BF16)
        ordered = dot(order, cells)
        store_quarters(ordered, entering, level, width, pieces)
        edges(ordered, level)
        ready(level)


def attended(q, k, v, bias, head_size):
    cells = q.shape[0]
    first = iota((cells, PAIR), 1) < head_size
    ones = jnp.ones((cells, PAIR), BF16)
    pairs = [slice(p * PAIR, (p + 1) * PAIR) for p in range(q.shape[1] // PAIR)]
    scores = []
    for pair in pairs:
        zero = jnp.zeros((cells, PAIR), F32)
        both = jnp.concatenate([jnp.where(first, q[:, pair], zero), jnp.where(first, zero, q[:, pair])], axis=0)
        scores.append(lax.dot_general(both.astype(BF16), k[:, pair].astype(BF16), NT, preferred_element_type=F32))
    weights = []
    for score in scores:
        score = score + bias
        weights.append(jnp.exp(score - jnp.max(score, axis=-1, keepdims=True)).astype(BF16))
    sums = [
        dot(weight, jnp.concatenate([v[:, pair].astype(BF16), ones], axis=1))
        for weight, pair in zip(weights, pairs)
    ]
    parts = []
    for both in sums:
        value = jnp.where(first, both[:cells, :PAIR], both[cells:, :PAIR])
        total = jnp.where(first, both[:cells, PAIR:], both[cells:, PAIR:])
        parts.append((value / total).astype(BF16))
    return jnp.concatenate(parts, axis=1)


def section(x, bias, wqkv, wout, gain):
    width = x.shape[1]
    head_size = width // HEADS
    q = dot(x, wqkv[:, :width]) * (1.0 / math.sqrt(head_size))
    k = dot(x, wqkv[:, width : 2 * width])
    v = dot(x, wqkv[:, 2 * width :])
    projected = dot(attended(q, k, v, bias, head_size), wout[...])
    centered = projected - jnp.mean(projected, axis=-1, keepdims=True)
    variance = jnp.mean(centered * centered, axis=-1, keepdims=True)
    branch = centered * lax.rsqrt(variance + 1e-05) * gain
    return x.astype(F32) + branch


def kernel(
    lat_signs, lon_signs, small_step, line_counts,
    offsets_hbm, latents_hbm, mask_hbm, embed_hbm, wqkv_hbm, wout_hbm, gain_hbm, out_ref,
    offsets_ref, latents_ref, mask_ref, embed_ref, gain_ref,
    entering, leaving, far_entering, far_leaving, lines, corners, wqkv, wout,
    main_in, tail_in, far_in, main_out, tail_out, far_out, bias, total,
    load_sem, send_sem, recv_sem, cross_send, cross_recv,
):
    segment, lon, lat = (lax.axis_index(axis) for axis in ("segment", "lon", "lat"))
    lons, lats = lax.axis_size("lon"), lax.axis_size("lat")
    levels, width = latents_ref.shape[2:]
    pieces = width // PAIR
    at = lambda a, b: (segment, lax.rem(lon + b + lons, lons), lax.rem(lat + a + lats, lats))
    pick = lambda pair: pair[0] + segment * (pair[1] - pair[0])

    across = (1 - segment, lon, lat)
    own_signs = tuple(-sign for sign in lat_signs[1])
    edge_of = lambda sign: lats - 1 if sign < 0 else 0
    edges_at = tuple(edge_of(sign) for sign in own_signs)
    on_edge = lat == pick(edges_at)
    on_first_edge = lat == edges_at[0]
    extra = max(line_counts)
    barrier = pltpu.get_barrier_semaphore()

    def greet(partner):
        pl.semaphore_signal(barrier, inc=1, device_id=partner, device_id_type=pl.DeviceIdType.MESH)

    for partner in (at(0, -1), at(0, 1), across):
        greet(partner)
    for a in (-1, 1):
        def greet_row():
            for b in (-1, 0, 1):
                greet(at(a, b))

        if extra:
            pl.when((lat + a >= 0) & (lat + a < lats))(greet_row)
        else:
            greet_row()

    greetings = 9
    if extra:
        greetings = 3 + 3 * ((lat > 0).astype(jnp.int32) + (lat < lats - 1).astype(jnp.int32))

    def load(slot, source_ref, target_ref):
        return pltpu.make_async_copy(source_ref, target_ref, load_sem.at[slot])

    seeds = [load(0, latents_hbm, latents_ref), load(1, mask_hbm, mask_ref), load(2, embed_hbm, embed_ref)]
    shifts, gains = load(3, offsets_hbm, offsets_ref), load(4, gain_hbm, gain_ref)
    weights = [load(5, wqkv_hbm.at[0], wqkv), load(6, wout_hbm.at[0], wout)]

    @pl.when(segment == 0)
    def _():
        for copy in seeds:
            copy.start()

    for copy in (shifts, gains, *weights):
        copy.start()

    on_small = segment == small_step
    edge_lat, edge_lon = lat_signs[small_step][small_step], lon_signs[small_step][small_step]

    def small_exchange(ref, level):
        low, right = at(-edge_lat, 0), at(0, -edge_lon)
        plan = (
            (0, lines.at[level, pl.ds(0, QUAD)], (pl.ds(4 * QUAD, QUAD), pl.ds(0, width)), low),
            (1, lines.at[level, pl.ds(QUAD, QUAD)], (pl.ds(6 * QUAD, QUAD), pl.ds(0, width)), right),
            (3, corners.at[level], (pl.ds(8 * QUAD, QUAD), pl.ds(width, PAIR)), at(-edge_lat, -edge_lon)),
        )
        return [
            pltpu.make_async_remote_copy(
                src_ref=held,
                dst_ref=ref.at[level, *target],
                send_sem=send_sem.at[small_step, level, slot],
                recv_sem=recv_sem.at[small_step, level, slot],
                device_id=device,
                device_id_type=pl.DeviceIdType.MESH,
            )
            for slot, held, target, device in plan
        ]

    def edges(cells, level):
        store_edges(cells, edge_lat, edge_lon, lines, corners, level, pieces)

    @pl.when(on_small)
    def _():
        ref = (entering, leaving)[small_step]
        for level in range(levels):
            for start in (5 * QUAD, 7 * QUAD):
                ref[level, pl.ds(start, QUAD), :] = jnp.zeros((QUAD, width + PAIR), BF16)
            for start in (4 * QUAD, 6 * QUAD):
                ref[level, pl.ds(start, QUAD), pl.ds(width, PAIR)] = jnp.zeros((QUAD, PAIR), BF16)
            ref[level, pl.ds(8 * QUAD, QUAD), pl.ds(0, width)] = jnp.zeros((QUAD, width), BF16)

    crossed = QUAD * line_counts[0]
    far_here = (segment == 1) & on_first_edge

    def clear(level):
        for index, ref in enumerate((entering, leaving)):
            behind = lat + pick(lat_signs[index])

            @pl.when((behind < 0) | (behind >= lats))
            def _():
                for start, count in ((4 * QUAD, 2 * QUAD), (8 * QUAD, QUAD)):
                    ref[level, pl.ds(start, count), :] = jnp.zeros((count, width + PAIR), BF16)

        for start in (0, QUAD * extra):
            @pl.when(jnp.logical_not(far_here))
            def _():
                far_entering[level, pl.ds(start, crossed), :] = jnp.zeros((crossed, width), BF16)

            if crossed < QUAD * extra:
                left = QUAD * extra - crossed
                far_entering[level, pl.ds(start + crossed, left), :] = jnp.zeros((left, width), BF16)

        @pl.when(jnp.logical_not(on_edge))
        def _():
            far_leaving[level, pl.ds(QUAD * extra, QUAD * extra), :] = jnp.zeros((QUAD * extra, width), BF16)

    def far_exchange(index, level):
        ref, count = ((far_entering, crossed), (far_leaving, QUAD * extra))[index]
        return pltpu.make_async_remote_copy(
            src_ref=ref.at[level, pl.ds(0, count)],
            dst_ref=ref.at[level, pl.ds(QUAD * extra, count)],
            send_sem=send_sem.at[index, level, 4],
            recv_sem=recv_sem.at[index, level, 4],
            device_id=at(0, -pick(lon_signs[index])),
            device_id_type=pl.DeviceIdType.MESH,
        )

    def exchange(index, ref, level):
        a, b = pick(lat_signs[index]), pick(lon_signs[index])
        low, right = (1 - a) // 2, (1 - b) // 2
        plan = (
            (2 * QUAD * low, 2 * QUAD, 4 * QUAD, at(-a, 0)),
            (QUAD * right, QUAD, 6 * QUAD, at(0, -b)),
            (2 * QUAD + QUAD * right, QUAD, 7 * QUAD, at(0, -b)),
            (2 * QUAD * low + QUAD * right, QUAD, 8 * QUAD, at(-a, -b)),
        )
        return [
            pltpu.make_async_remote_copy(
                src_ref=ref.at[level, pl.ds(pl.multiple_of(start, QUAD), count)],
                dst_ref=ref.at[level, pl.ds(target, count)],
                send_sem=send_sem.at[index, level, slot],
                recv_sem=recv_sem.at[index, level, slot],
                device_id=device,
                device_id_type=pl.DeviceIdType.MESH,
            )
            for slot, (start, count, target, device) in enumerate(plan)
        ]

    def guarded(copies, other, act, far_slots):
        inside = (other >= 0) & (other < lats)
        for slot, copy in enumerate(copies):
            if extra and slot in far_slots:
                pl.when(inside)(functools.partial(act, copy))
            else:
                act(copy)

    def each_transfer(index, level, act, way):
        ref = (entering, leaving)[index]

        def whole():
            guarded(exchange(index, ref, level), lat + way * pick(lat_signs[index]), act, (0, 3))

        def edge():
            guarded(small_exchange(ref, level), lat + way * edge_lat, act, (0, 2))

        if index == small_step:
            pl.when(on_small)(edge)
            pl.when(jnp.logical_not(on_small))(whole)
        else:
            whole()
        if extra:
            pl.when(far_here if index == 0 else on_edge)(lambda: act(far_exchange(index, level)))

    low_next = (1 - lat_signs[0][1]) // 2

    def crossing(level, part):
        if part == 2:
            rows, held, target = pl.ds(0, crossed), far_leaving, far_entering
        else:
            rows = pl.ds(2 * QUAD * (low_next if part == 0 else 1 - low_next), 2 * QUAD)
            held, target = leaving, entering
        return pltpu.make_async_remote_copy(
            src_ref=held.at[level, rows],
            dst_ref=target.at[level, rows],
            send_sem=cross_send.at[level, part],
            recv_sem=cross_recv.at[level, part],
            device_id=across,
            device_id_type=pl.DeviceIdType.MESH,
        )

    def each_crossing(level, act):
        act(crossing(level, 0))
        if extra:
            pl.when(on_first_edge)(lambda: act(crossing(level, 2)))
        act(crossing(level, 1))

    def each_level(step):
        def run(level, carry):
            step(level)
            return carry

        lax.fori_loop(0, levels, run, 0)

    def enter(level):
        each_transfer(0, level, lambda copy: copy.start(), -1)

    def ready(level):
        if level == 0:
            pl.semaphore_wait(barrier, greetings)
        enter(level)

    @pl.when(segment == 1)
    def _():
        pl.semaphore_wait(barrier, greetings)

    @pl.when(segment == 0)
    def _():
        for copy in seeds:
            copy.wait()
        seed(
            entering, latents_ref, mask_ref, embed_ref, pieces,
            edges if small_step == 0 else lambda cells, level: None, ready,
        )

    if extra:
        each_level(clear)
    shifts.wait()
    lat_base = [based(offsets_ref[s, 0], WLAT) for s in (0, 1)]
    lon_base = [based(offsets_ref[s, 1], WLON) for s in (0, 1)]
    first = segment == 0
    lat_own, lon_own = jnp.where(first, lat_base[0], lat_base[1]), jnp.where(first, lon_base[0], lon_base[1])
    lat_from, lon_from = jnp.where(first, 0, lat_base[0]), jnp.where(first, 0, lon_base[0])
    own_sign = pick(own_signs)
    offset = jnp.where(first, offsets_ref[0, 0], offsets_ref[1, 0])
    count = HELD + QUAD * extra

    def targets(shape, axis):
        t = iota(shape, axis)
        row, column = quarter_cell(t)
        ground = row + lat_own + lat * WLAT
        if not extra:
            ground = jnp.where(ground < 0, ground + lats * WLAT, ground)
            ground = jnp.where(ground >= lats * WLAT, ground - lats * WLAT, ground)
            live = t < CELLS
            group = jnp.where(live, (ground < offset).astype(jnp.int32), 2)
            return row + lat_own, column + lon_own, live, group
        outside = t >= HELD
        line, place = (t - HELD) >> 4, (t - HELD) & (QUAD - 1)
        edge_row = jnp.where(own_sign < 0, WLAT - 1 - line, line)
        row = jnp.where(outside, edge_row, row + lat_own)
        column = jnp.where(outside, place, column) + lon_own
        kept = on_edge & (place < WLON) & (line < jnp.abs(lat_own))
        live = (outside & kept) | ((t < CELLS) & (ground >= 0) & (ground < lats * WLAT))
        group = jnp.where(live, outside.astype(jnp.int32), 2)
        return row, column, live, group

    def beyond(row, held_sign, held_base):
        if not extra:
            return None
        line = row + held_base
        line = jnp.where(held_sign < 0, WLAT - 1 - line, line)
        past = ((row < 0) & (lat == 0)) | ((row >= WLAT) & (lat == lats - 1))
        return extra, line, past

    row, column, live, group = targets((count, 1), 0)
    row, column = row - lat_from, column - lon_from
    choosers(
        row, column, (pick(lat_signs[0]), pick(lon_signs[0])), on_small if small_step == 0 else None,
        beyond(row, own_signs[0], lat_base[0]), live, pieces, main_in, tail_in, far_in,
    )
    _, _, _, group_across = targets((1, count), 1)
    excluded = jnp.where(group == group_across, 0.0, -1e30)
    bias[pl.ds(0, count), :] = excluded
    bias[pl.ds(count, count), :] = excluded

    place = iota((CELLS * levels, 1), 0)
    row, column = split_by(place, WLON * levels, WLAT)
    column, held_level = split_by(column, levels, WLON)
    row, column = row - lat_own, column - lon_own

    def choose_leaving(level):
        choosers(
            row, column, (pick(lat_signs[1]), pick(lon_signs[1])), on_small if small_step == 1 else None,
            beyond(row, own_sign, lat_own), held_level == level, pieces,
            main_out.at[level], tail_out.at[level], far_out.at[level],
        )

    each_level(choose_leaving)
    gains.wait()
    for copy in weights:
        copy.wait()

    @pl.when(segment == 1)
    def _():
        def forward(level):
            copies = exchange(0, entering, level)
            start = lambda copy: copy.start()
            crossing(level, 0).wait_recv()
            guarded([copies[0], copies[3]], lat - lat_signs[0][1], start, (0, 1))
            copies[1 + low_next].start()

            if extra:
                @pl.when(on_first_edge)
                def _():
                    crossing(level, 2).wait_recv()
                    far_exchange(0, level).start()

            crossing(level, 1).wait_recv()
            copies[2 - low_next].start()

        each_level(forward)

    gain = jnp.where(first, gain_ref[0:1, :], gain_ref[1:2, :])

    def work(level):
        each_transfer(0, level, lambda copy: copy.wait_recv(), 1)
        x = gathered(entering[level], far_entering[level] if extra else None, main_in, tail_in, far_in, width, pieces).astype(BF16)
        cells = section(x, bias[...], wqkv, wout, gain)
        store_quarters(cells, leaving, level, width, pieces)
        if extra:
            far_leaving[level, pl.ds(0, QUAD * extra), :] = cells[HELD:].astype(BF16)

        @pl.when(segment == 0)
        def _():
            each_crossing(level, lambda copy: copy.start())

        if small_step == 1:
            pl.when(on_small)(lambda: edges(cells, level))
        each_transfer(1, level, lambda copy: copy.start(), -1)

    each_level(work)

    total[...] = jnp.zeros_like(total)

    def finish(level):
        each_transfer(1, level, lambda copy: copy.wait_recv(), 1)
        total[...] += gathered(
            leaving[level], far_leaving[level] if extra else None,
            main_out.at[level], tail_out.at[level], far_out.at[level], width, pieces,
        )

    each_level(finish)
    out_ref[...] = total[...].astype(BF16).reshape(out_ref.shape)

    def settle(level):
        for index in (0, 1):
            each_transfer(index, level, lambda copy: copy.wait_send(), -1)

        @pl.when(segment == 0)
        def _():
            each_crossing(level, lambda copy: copy.wait_send())

    each_level(settle)


def sections(variant, offsets, latents, land_mask, land_embed, qkv_weight, out_weight, norm_gain):
    _, _, levels, width = latents.shape
    second_known = variant >= 4
    signs = []
    for bit in (2, 1):
        other = -1 if variant & bit else 1
        if second_known:
            entering, leaving = (other, -other), (-other, 1)
        else:
            entering, leaving = (-1, other), (1, -other)
        signs.append((entering, leaving))
    if not second_known:
        line_counts = (1, HALF_LAT if signs[0][1][1] > 0 else HALF_LAT - 1)
    elif signs[0][0][0] > 0:
        line_counts = (HALF_LAT - 1, 1)
    else:
        line_counts = (0, 0)
    extra = max(line_counts)
    count = HELD + QUAD * extra
    far_rows = 2 * QUAD * max(extra, 1)
    far_block = (levels, far_rows, width)
    pieces = width // PAIR
    in_vmem = pl.BlockSpec(memory_space=pltpu.VMEM)
    in_hbm = pl.BlockSpec(memory_space=pl.ANY)
    block = (levels, 9 * QUAD, width + PAIR)
    return pl.pallas_call(
        functools.partial(kernel, signs[0], signs[1], int(second_known), line_counts),
        out_shape=jax.ShapeDtypeStruct(latents.shape, BF16),
        in_specs=[in_hbm] * 7,
        out_specs=in_vmem,
        scratch_shapes=[
            pltpu.SMEM(offsets.shape, offsets.dtype),
            pltpu.VMEM(latents.shape, latents.dtype),
            pltpu.VMEM(land_mask.shape, land_mask.dtype),
            pltpu.VMEM(land_embed.shape, land_embed.dtype),
            pltpu.VMEM(norm_gain.shape, norm_gain.dtype),
            pltpu.VMEM(block, BF16),
            pltpu.VMEM(block, BF16),
            pltpu.VMEM(far_block, BF16),
            pltpu.VMEM(far_block, BF16),
            pltpu.VMEM((levels, 2 * QUAD, width), BF16),
            pltpu.VMEM((levels, QUAD, PAIR), BF16),
            pltpu.VMEM(qkv_weight.shape[1:], BF16),
            pltpu.VMEM(out_weight.shape[1:], BF16),
            pltpu.VMEM((count, 9 * QUAD), BF16),
            pltpu.VMEM((count * pieces, 9 * QUAD), BF16),
            pltpu.VMEM((count, far_rows), BF16),
            pltpu.VMEM((levels, CELLS * levels, 9 * QUAD), BF16),
            pltpu.VMEM((levels, CELLS * levels * pieces, 9 * QUAD), BF16),
            pltpu.VMEM((levels, CELLS * levels, far_rows), BF16),
            pltpu.VMEM((2 * count, count), F32),
            pltpu.VMEM((CELLS * levels, width), F32),
            pltpu.SemaphoreType.DMA((7,)),
            pltpu.SemaphoreType.DMA((2, levels, 5)),
            pltpu.SemaphoreType.DMA((2, levels, 5)),
            pltpu.SemaphoreType.DMA((levels, 3)),
            pltpu.SemaphoreType.DMA((levels, 3)),
        ],
        compiler_params=pltpu.CompilerParams(
            collective_id=variant, has_side_effects=True, vmem_limit_bytes=48 * 1024 * 1024
        ),
    )(offsets, latents, land_mask, land_embed, qkv_weight, out_weight, norm_gain)


def variant_kernel(offsets_ref, variant_ref):
    shifts = [(offsets_ref[s, 0], offsets_ref[s, 1]) for s in (0, 1)]
    signs = [
        2 * (a >= HALF_LAT).astype(jnp.int32) + (b >= HALF_LON).astype(jnp.int32) for a, b in shifts
    ]
    known = (shifts[0][0] == WLAT - 1) & (shifts[0][1] == WLON - 1)
    variant_ref[0] = jnp.where(known, signs[1], 4 + signs[0])


def body(latents, land_mask, land_embed, qkv_weight, out_weight, norm_gain, offsets):
    assert latents.shape[1:3] == (WLAT, WLON)
    variant = pl.pallas_call(
        variant_kernel,
        out_shape=jax.ShapeDtypeStruct((1,), jnp.int32),
        in_specs=[pl.BlockSpec(memory_space=pltpu.SMEM)],
        out_specs=pl.BlockSpec(memory_space=pltpu.SMEM),
    )(offsets).reshape(())
    ways = [functools.partial(sections, v) for v in range(8)]
    out = lax.switch(
        variant, ways,
        offsets, latents.transpose(1, 2, 0, 3), land_mask, land_embed, qkv_weight, out_weight, norm_gain,
    )
    return out.transpose(2, 0, 1, 3)[None]


def solution(mesh):
    return jax.shard_map(
        body,
        mesh=mesh,
        in_specs=(
            P(None, "lat", "lon", None),
            P("lat", "lon"),
            P(),
            P("segment", None, None),
            P("segment", None, None),
            P(),
            P(),
        ),
        out_specs=P("segment", None, "lat", "lon", None),
        check_vma=False,
    )
```

profile of v0, /device:TPU:5, one launch (start us, length us, event | category | flops | bytes accessed | tf_op | source)
XLA Modules:
  0.0 32.0 jit_solution(11541909736804732242)
XLA Ops:
  0.0 1.2 %shard_map.73 = s32[1]{0:T(128)} custom-call(s32[2,2]{1,0:T(2,128)} %offsets_ref.1), custom_call_target="tpu_custom_call" | custom-call | tf_op jit(solution)/shard_map/pallas_call | solution.py:625
  1.9 29.4 %conditional.1 = (bf16[6,12,2,1024]{3,2,1,0:T(2,128)(2,1)S(1)}) conditional(s32[]{:T(128)} %bitcast, (s32[2,2]{1,0:T(2,128)}, bf16[6,12,2,1024]{3,2,1,0:T(2,128)(2,1)}, s32[6,12]{1,0:T(8,128)}, bf16[1024]{0:T(1024)(128)(2,1)}, bf16[1,1024,3072]{2,1,0:T(8,128)(2,1)}, /*index=5*/bf16[1,1024,1024]{2,1,0:T(8,128)(2,1)}, ...), branch_computations={%region_0.0_spmd, %region_1.0_spmd, %region_2.0_spmd, %region_3.0_... | conditional | bytes 8 | solution.py:632
  2.2 29.1 %branch_4_fun.1 = bf16[6,12,2,1024]{3,2,1,0:T(2,128)(2,1)S(1)} custom-call(s32[2,2]{1,0:T(2,128)} %get-tuple-element.154.offsets_hbm, bf16[6,12,2,1024]{3,2,1,0:T(2,128)(2,1)} %get-tuple-element.155.latents_hbm, s32[6,12]{1,0:T(8,128)} %get-tuple-element.156.mask_hbm, bf16[1024]{0:T(1024)(128)(2,1)} %get-tuple-element.157.embed_hbm, ...), custom_call_target="tpu_custom_call" | custom-call | tf_op jit(solution)/shard_map/cond/branch_4_fun/pallas_call | solution.py:575
  31.3 0.7 %copy.17 = bf16[1,2,6,12,1024]{4,1,3,2,0:T(2,128)(2,1)} copy(bf16[1,2,6,12,1024]{4,1,3,2,0:T(2,128)(2,1)S(1)} %bitcast.13) | data formatting | bytes 589824
where the time goes:
time: 32 us
  Pallas kernels  30.3 us (95%)
  local copies, waits for them, and re-layouts  0.72 us (2%)
  between operations  0.67 us (2%)
    pallas_call x1, Pallas kernels, sections(): pl.pallas_call(functools.partial(kernel, signs[0], signs[1], int(second_k...  29.1 us
    pallas_call x1, Pallas kernels, body(): pl.pallas_call(variant_kernel, out_shape=jax.ShapeDtypeStruct((1,), jnp.i...  1.21 us
    unnamed x1, local copies, waits for them, and re-layouts  0.72 us

commit v1 on v0

--- a/solution.py
+++ b/solution.py
@@ -322,22 +322,24 @@
     def exchange(index, ref, level):
         a, b = pick(lat_signs[index]), pick(lon_signs[index])
         low, right = (1 - a) // 2, (1 - b) // 2
+        piece = QUAD * right
         plan = (
-            (2 * QUAD * low, 2 * QUAD, 4 * QUAD, at(-a, 0)),
-            (QUAD * right, QUAD, 6 * QUAD, at(0, -b)),
-            (2 * QUAD + QUAD * right, QUAD, 7 * QUAD, at(0, -b)),
-            (2 * QUAD * low + QUAD * right, QUAD, 8 * QUAD, at(-a, -b)),
+            (0, 2 * QUAD * low + piece, 4 * QUAD + piece, at(-a, 0)),
+            (1, piece, 6 * QUAD, at(0, -b)),
+            (2, 2 * QUAD + piece, 7 * QUAD, at(0, -b)),
+            (3, 2 * QUAD * low + piece, 8 * QUAD, at(-a, -b)),
+            (5, 2 * QUAD * low + QUAD - piece, 5 * QUAD - piece, at(-a, 0)),
         )
         return [
             pltpu.make_async_remote_copy(
-                src_ref=ref.at[level, pl.ds(pl.multiple_of(start, QUAD), count)],
-                dst_ref=ref.at[level, pl.ds(target, count)],
+                src_ref=ref.at[level, pl.ds(pl.multiple_of(start, QUAD), QUAD)],
+                dst_ref=ref.at[level, pl.ds(pl.multiple_of(target, QUAD), QUAD)],
                 send_sem=send_sem.at[index, level, slot],
                 recv_sem=recv_sem.at[index, level, slot],
                 device_id=device,
                 device_id_type=pl.DeviceIdType.MESH,
             )
-            for slot, (start, count, target, device) in enumerate(plan)
+            for slot, start, target, device in plan
         ]
 
     def guarded(copies, other, act, far_slots):
@@ -352,7 +354,7 @@
         ref = (entering, leaving)[index]
 
         def whole():
-            guarded(exchange(index, ref, level), lat + way * pick(lat_signs[index]), act, (0, 3))
+            guarded(exchange(index, ref, level), lat + way * pick(lat_signs[index]), act, (0, 3, 4))
 
         def edge():
             guarded(small_exchange(ref, level), lat + way * edge_lat, act, (0, 2))
@@ -365,13 +367,19 @@
         if extra:
             pl.when(far_here if index == 0 else on_edge)(lambda: act(far_exchange(index, level)))
 
-    low_next = (1 - lat_signs[0][1]) // 2
+    low_next, right_next = (1 - lat_signs[0][1]) // 2, (1 - lon_signs[0][1]) // 2
 
     def crossing(level, part):
         if part == 2:
             rows, held, target = pl.ds(0, crossed), far_leaving, far_entering
         else:
-            rows = pl.ds(2 * QUAD * (low_next if part == 0 else 1 - low_next), 2 * QUAD)
+            start, many = (
+                (2 * QUAD * low_next + QUAD * right_next, QUAD),
+                (2 * QUAD * low_next + QUAD * (1 - right_next), QUAD),
+                None,
+                (2 * QUAD * (1 - low_next), 2 * QUAD),
+            )[part]
+            rows = pl.ds(start, many)
             held, target = leaving, entering
         return pltpu.make_async_remote_copy(
             src_ref=held.at[level, rows],
@@ -384,9 +392,10 @@
 
     def each_crossing(level, act):
         act(crossing(level, 0))
+        act(crossing(level, 1))
         if extra:
             pl.when(on_first_edge)(lambda: act(crossing(level, 2)))
-        act(crossing(level, 1))
+        act(crossing(level, 3))
 
     def each_level(step):
         def run(level, carry):
@@ -492,6 +501,8 @@
             crossing(level, 0).wait_recv()
             guarded([copies[0], copies[3]], lat - lat_signs[0][1], start, (0, 1))
             copies[1 + low_next].start()
+            crossing(level, 1).wait_recv()
+            guarded([copies[4]], lat - lat_signs[0][1], start, (0,))
 
             if extra:
                 @pl.when(on_first_edge)
@@ -499,7 +510,7 @@
                     crossing(level, 2).wait_recv()
                     far_exchange(0, level).start()
 
-            crossing(level, 1).wait_recv()
+            crossing(level, 3).wait_recv()
             copies[2 - low_next].start()
 
         each_level(forward)
@@ -600,10 +611,10 @@
             pltpu.VMEM((2 * count, count), F32),
             pltpu.VMEM((CELLS * levels, width), F32),
             pltpu.SemaphoreType.DMA((7,)),
-            pltpu.SemaphoreType.DMA((2, levels, 5)),
-            pltpu.SemaphoreType.DMA((2, levels, 5)),
-            pltpu.SemaphoreType.DMA((levels, 3)),
-            pltpu.SemaphoreType.DMA((levels, 3)),
+            pltpu.SemaphoreType.DMA((2, levels, 6)),
+            pltpu.SemaphoreType.DMA((2, levels, 6)),
+            pltpu.SemaphoreType.DMA((levels, 4)),
+            pltpu.SemaphoreType.DMA((levels, 4)),
         ],
         compiler_params=pltpu.CompilerParams(
             collective_id=variant, has_side_effects=True, vmem_limit_bytes=48 * 1024 * 1024

time: 32 us -> 32.4 us (1.012); the launches traced: 32 us -> 32 us
  loops' own time: 0.31 us -> 0.65 us
    another operation x1, loops' own time: 0.31 us -> 0.65 us  [body(): lax.switch(variant, ways, offsets, latents.transpose(1, 2, 0, 3), land_ma...]
    pallas_call x1, Pallas kernels: 29.1 us -> 28.8 us  [sections(): pl.pallas_call(functools.partial(kernel, signs[0], signs[1], int(second_k...]
where the time goes in v1:
time: 32.4 us; the launch traced here: 32 us
  Pallas kernels  30 us (93%)
  local copies, waits for them, and re-layouts  0.72 us (2%)
  between operations  0.67 us (2%)
  loops' own time  0.65 us (2%)
    pallas_call x1, Pallas kernels, sections(): pl.pallas_call(functools.partial(kernel, signs[0], signs[1], int(second_k...  28.8 us
    pallas_call x1, Pallas kernels, body(): pl.pallas_call(variant_kernel, out_shape=jax.ShapeDtypeStruct((1,), jnp.i...  1.21 us
    unnamed x1, local copies, waits for them, and re-layouts  0.72 us

profile of v1, /device:TPU:5, one launch (start us, length us, event | category | flops | bytes accessed | tf_op | source)
XLA Modules:
  0.0 32.0 jit_solution(17274488526136469081)
XLA Ops:
  0.0 1.2 %shard_map.73 = s32[1]{0:T(128)} custom-call(s32[2,2]{1,0:T(2,128)} %offsets_ref.1), custom_call_target="tpu_custom_call" | custom-call | tf_op jit(solution)/shard_map/pallas_call | solution.py:636
  1.9 29.5 %conditional.1 = (bf16[6,12,2,1024]{3,2,1,0:T(2,128)(2,1)S(1)}) conditional(s32[]{:T(128)} %bitcast, (s32[2,2]{1,0:T(2,128)}, bf16[6,12,2,1024]{3,2,1,0:T(2,128)(2,1)}, s32[6,12]{1,0:T(8,128)}, bf16[1024]{0:T(1024)(128)(2,1)}, bf16[1,1024,3072]{2,1,0:T(8,128)(2,1)}, /*index=5*/bf16[1,1024,1024]{2,1,0:T(8,128)(2,1)}, ...), branch_computations={%region_0.0_spmd, %region_1.0_spmd, %region_2.0_spmd, %region_3.0_... | conditional | bytes 8 | solution.py:643
  2.2 28.8 %branch_5_fun.1 = bf16[6,12,2,1024]{3,2,1,0:T(2,128)(2,1)S(1)} custom-call(s32[2,2]{1,0:T(2,128)} %get-tuple-element.161.offsets_hbm, bf16[6,12,2,1024]{3,2,1,0:T(2,128)(2,1)} %get-tuple-element.162.latents_hbm, s32[6,12]{1,0:T(8,128)} %get-tuple-element.163.mask_hbm, bf16[1024]{0:T(1024)(128)(2,1)} %get-tuple-element.164.embed_hbm, ...), custom_call_target="tpu_custom_call" | custom-call | tf_op jit(solution)/shard_map/cond/branch_5_fun/pallas_call | solution.py:586
  31.3 0.7 %copy.17 = bf16[1,2,6,12,1024]{4,1,3,2,0:T(2,128)(2,1)} copy(bf16[1,2,6,12,1024]{4,1,3,2,0:T(2,128)(2,1)S(1)} %bitcast.13) | data formatting | bytes 589824
